TPU v7x, 32 devices: a whole 2x2x4 slice. The times are simulated.
32 devices in a mesh: grp: 4 (over y, x), dev: 8 (over z, core).
Axes of the slice: x: 2, y: 2, z: 4, core: 2. Of those that a mesh axis runs over, the one named last changes fastest.
Arguments:
- block_values: bfloat16 [384, 9, 128, 128], P(('grp', 'dev')), may hold values from -0.1875 to 0.1875
- block_columns: int32 [384, 9], P(('grp', 'dev')), may hold values from 0 to 17, as said below
- tentative: bfloat16 [384, 128, 128], P(('grp', 'dev')), may hold values from -1.1953125 to 1.1953125
- inverse_diagonal: bfloat16 [384, 128, 128], P(('grp', 'dev')), may hold values from -0.5 to 0.5
- aggregate: int32 [384], P(('grp', 'dev')), may hold values from 0 to 1, as said below
- ghost_rows: int32 [32, 2, 3], P(('grp', 'dev')), may hold values from 0 to 11, as said below
- damping: float32 [1], replicated, may hold values from 0.5 to 0.8
Outputs:
- coarse_op: bfloat16 [64, 128, 1792], P(('grp', 'dev'))
Inputs may be any that keep to these rules, and one draw needn't show every extreme that they name: `block_columns`: in part n, row r names its own row r first; the 9 entries of a row differ; entries from 12 to 14 never stand in the first part, entries from 15 on never in the last. `aggregate`: each of the 2 aggregates of a part holds one or more of its rows. `ghost_rows`: the 3 rows of each list differ.
All inputs are finite; a program needn't handle non-finite values.
Results may differ from a plain program's by a relative error of at most 0.0068.
Values may be sent and summed in bfloat16 or wider, within the bound.
A program may use at most 64 MiB of HBM per device.

v0:
```python
import jax
import jax.numpy as jnp
from jax import lax
from jax.sharding import PartitionSpec as P

CA = 2


def from_behind(block, axis, distance):
    devices = range(lax.axis_size(axis))
    route = [(i - distance, i) for i in devices if i - distance in devices]
    return lax.ppermute(block, axis, route)


def place_own(tentative, aggregate):
    aggregate_mask = aggregate[:, None] == jnp.arange(CA, dtype=jnp.int32)[None, :]
    spread = jnp.where(
        aggregate_mask[:, None, :, None], tentative[:, :, None, :], jnp.zeros((), tentative.dtype)
    )
    return spread.reshape(tentative.shape[0], tentative.shape[1], CA * tentative.shape[2])


def dense_rows(values, columns, lookup_rows):
    selector = (
        columns[:, :, None] == jnp.arange(lookup_rows, dtype=jnp.int32)[None, None, :]
    ).astype(values.dtype)
    return jnp.einsum(
        "rkl,rkab->rlab", selector, values, preferred_element_type=jnp.float32
    ).astype(values.dtype)


def assemble(dense, own_count, ghost_count, lookup, block_span):
    width = lookup.shape[2]
    middle = jnp.einsum(
        "rlab,lbc->rac",
        dense[:, :own_count],
        lookup[:own_count],
        preferred_element_type=jnp.float32,
    )
    left = jnp.einsum(
        "rlab,lbc->rac",
        dense[:, own_count : own_count + ghost_count],
        lookup[own_count : own_count + ghost_count],
        preferred_element_type=jnp.float32,
    )
    right = jnp.einsum(
        "rlab,lbc->rac",
        dense[:, own_count + ghost_count :],
        lookup[own_count + ghost_count :],
        preferred_element_type=jnp.float32,
    )
    total = jnp.pad(middle, ((0, 0), (0, 0), (block_span, block_span)))
    total = total.at[:, :, :width].add(left)
    total = total.at[:, :, 2 * block_span :].add(right)
    return total


def wanted_list(payload, offset):
    return from_behind(payload, ("grp", "dev"), offset)


def rim_tentative(payload, offset):
    return from_behind(payload, ("grp", "dev"), offset)


def rim_smoothed(payload, offset):
    return from_behind(payload, ("grp", "dev"), offset)


def coarse_part(payload, offset):
    return from_behind(payload.astype(jnp.bfloat16), ("grp", "dev"), offset).astype(payload.dtype)


def shards(
    block_values, block_columns, tentative, inverse_diagonal, aggregate, ghost_rows, damping
):
    row_count = block_columns.shape[0]
    block_width = tentative.shape[1]
    list_length = ghost_rows.shape[2]
    block_span = CA * block_width
    ghost_lists = ghost_rows[0]
    own_rows = place_own(tentative, aggregate)
    dense = dense_rows(block_values, block_columns, row_count + 2 * list_length)
    wanted_left = wanted_list(ghost_lists[1], 1)
    wanted_right = wanted_list(ghost_lists[0], -1)
    left_ghosts = rim_tentative(jnp.take(own_rows, wanted_right, axis=0), 1)
    right_ghosts = rim_tentative(jnp.take(own_rows, wanted_left, axis=0), -1)
    lookup = jnp.concatenate([own_rows, left_ghosts, right_ghosts], axis=0)
    smooth_sum = assemble(dense, row_count, list_length, lookup, block_span)
    smooth_half = smooth_sum.astype(jnp.bfloat16)
    scaled = jnp.einsum(
        "rab,rbc->rac", inverse_diagonal, smooth_half, preferred_element_type=jnp.float32
    )
    own_wide = jnp.pad(own_rows, ((0, 0), (0, 0), (block_span, block_span))).astype(jnp.float32)
    prolong = (own_wide - damping[0] * scaled).astype(jnp.bfloat16)
    left_smoothed = rim_smoothed(jnp.take(prolong, wanted_right, axis=0), 1)
    right_smoothed = rim_smoothed(jnp.take(prolong, wanted_left, axis=0), -1)
    prolong_lookup = jnp.concatenate([prolong, left_smoothed, right_smoothed], axis=0)
    applied = assemble(dense, row_count, list_length, prolong_lookup, block_span).astype(
        jnp.bfloat16
    )
    flat_prolong = prolong.reshape(row_count * block_width, 3 * block_span)
    flat_applied = applied.reshape(row_count * block_width, 5 * block_span)
    galerkin = lax.dot_general(
        flat_prolong, flat_applied, (((0,), (0,)), ((), ())), preferred_element_type=jnp.float32
    )
    from_right = coarse_part(galerkin[:block_span], -1)
    from_left = coarse_part(galerkin[2 * block_span :], 1)
    result = jnp.pad(galerkin[block_span : 2 * block_span], ((0, 0), (block_span, block_span)))
    result = result + jnp.pad(from_right, ((0, 0), (2 * block_span, 0)))
    result = result + jnp.pad(from_left, ((0, 0), (0, 2 * block_span)))
    return result.reshape(CA, block_width, 7 * block_span).astype(jnp.bfloat16)


def solution(mesh):
    return jax.shard_map(
        shards,
        mesh=mesh,
        in_specs=(
            P(("grp", "dev"), None, None, None),
            P(("grp", "dev"), None),
            P(("grp", "dev"), None, None),
            P(("grp", "dev"), None, None),
            P(("grp", "dev")),
            P(("grp", "dev"), None, None),
            P(),
        ),
        out_specs=P(("grp", "dev"), None, None),
        check_vma=False,
    )
```

profile of v0, /device:TPU:4, one launch (start us, length us, event | category | flops | bytes accessed | tf_op | source)
XLA Modules:
  0.0 123.1 jit_solution(9563505961598236245)
XLA Ops:
  0.0 1.4 %slice_bitcast_fusion = (s32[3]{0:T(128)}, s32[3]{0:T(128)S(1)}) fusion(s32[1,2,3]{2,1,0:T(2,128)} %param.24), kind=kLoop, calls=%fused_computation.52 | loop fusion | bytes 48 | tf_op jit(solution)/shard_map/squeeze | solution.py:84
  1.4 1.9 %collective-permute-start.2 = (s32[3]{0:T(128)}, s32[3]{0:T(128)S(1)}, u32[]{:S(2)}, u32[]{:S(2)}) collective-permute-start(s32[3]{0:T(128)} %get-tuple-element.59), channel_id=1, source_target_pairs={{0,1},{1,2},{2,3},{3,4},{4,5},{5,6},{6,7},{7,8},{8,9},{9,10},{10,1... | collective-permute-start | bytes 44 | tf_op jit(solution)/shard_map/ppermute | solution.py:12
  3.3 7.2 %collective-permute-start = (s32[3]{0:T(128)S(1)}, s32[3]{0:T(128)S(1)}, u32[]{:S(2)}, u32[]{:S(2)}) collective-permute-start(s32[3]{0:T(128)S(1)} %get-tuple-element.60), channel_id=1, source_target_pairs={{1,0},{2,1},{3,2},{4,3},{5,4},{6,5},{7,6},{8,7},{9,8},{10,9},{11,1... | collective-permute-start | bytes 44 | tf_op jit(solution)/shard_map/ppermute | solution.py:12
  10.6 5.1 %convolution_convert_fusion = bf16[12,18,128,128]{3,1,2,0:T(8,128)(2,1)S(1)} fusion(bf16[12,9,128,128]{3,2,1,0:T(8,128)(2,1)S(1)} %copy-done, s32[12,9]{1,0:T(8,128)} %param.20), kind=kOutput, calls=%fused_computation.4 | convolution fusion | flops 67241880 | bytes 10617264 | tf_op jit(solution)/shard_map/rkl,rkab->rlab/dot_general | solution.py:27
  15.7 3.4 %fusion.39 = (bf16[12,3,128,128]{3,1,2,0:T(4,128)(2,1)}, bf16[12,3,128,128]{3,1,2,0:T(4,128)(2,1)}) fusion(bf16[12,18,128,128]{3,1,2,0:T(8,128)(2,1)S(1)} %convolution_convert_fusion), kind=kLoop, calls=%fused_computation.54 | loop fusion | bytes 4718592 | tf_op jit(solution)/shard_map/slice | solution.py:48
  19.1 3.8 %slice.144 = bf16[12,12,128,128]{3,1,2,0:T(8,128)(2,1)} slice(bf16[12,18,128,128]{3,1,2,0:T(8,128)(2,1)S(1)} %convolution_convert_fusion), slice={[0:12], [0:12], [0:128], [0:128]} | slice | bytes 9437184 | tf_op jit(solution)/shard_map/slice | solution.py:36
  23.7 1.9 %copy.18 = bf16[12,128,128]{1,2,0:T(8,128)(2,1)} copy(bf16[12,128,128]{2,1,0:T(8,128)(2,1)} %param.21) | data formatting | bytes 786432 | tf_op args[2]
  25.7 2.2 %bitcast_select_fusion = bf16[12,128,256]{1,2,0:T(8,128)(2,1)} fusion(pred[12,256]{1,0:T(8,128)(4,1)S(1)} %bitcast.66, bf16[12,128,128]{1,2,0:T(8,128)(2,1)} %copy.18), kind=kLoop, calls=%fused_computation.33 | loop fusion | flops 393216 | bytes 1182720 | tf_op jit(solution)/shard_map/jit(_where)/select_n | solution.py:17
  27.9 2.3 %copy.22 = bf16[12,128,256]{2,1,0:T(8,128)(2,1)} copy(bf16[12,128,256]{1,2,0:T(8,128)(2,1)} %bitcast_select_fusion) | data formatting | bytes 1572864 | tf_op jit(solution)/shard_map/jit(_where)/select_n | solution.py:17
  30.2 4.4 %fusion.24 = f32[12,128,256]{2,1,0:T(8,128)S(1)} fusion(bf16[12,12,128,128]{3,1,2,0:T(8,128)(2,1)} %slice.144, bf16[12,128,256]{1,2,0:T(8,128)(2,1)} %bitcast_select_fusion), kind=kOutput, calls=%fused_computation.27 | convolution fusion | flops 1207959552 | bytes 7077888 | tf_op jit(solution)/shard_map/rlab,lbc->rac/dot_general | solution.py:34
  34.6 2.7 %pad.39 = f32[12,128,768]{2,1,0:T(8,128)} pad(f32[12,128,256]{2,1,0:T(8,128)S(1)} %fusion.24, f32[]{:T(128)} %constant.119.clone.1), padding=0_0x0_0x256_256 | pad | bytes 6291460 | tf_op jit(solution)/shard_map/jit(_pad)/pad | solution.py:52
  37.9 2.4 %gather_fusion.1 = bf16[3,128,256]{1,2,0:T(8,128)(2,1)} fusion(bf16[12,128,256]{1,2,0:T(8,128)(2,1)} %bitcast_select_fusion, s32[1024]{0:T(1024)S(1)} %pad_clamp_fusion), kind=kCustom, calls=%fused_computation.2.clone | custom fusion | bytes 393228 | tf_op jit(solution)/shard_map/jit(_take)/gather | solution.py:87
  40.3 2.4 %gather_fusion = bf16[3,128,256]{2,1,0:T(8,128)(2,1)} fusion(bf16[12,128,256]{2,1,0:T(8,128)(2,1)} %copy.22, s32[1024]{0:T(1024)S(1)} %pad_clamp_fusion.1), kind=kCustom, calls=%fused_computation.clone | custom fusion | bytes 393228 | tf_op jit(solution)/shard_map/jit(_take)/gather | solution.py:86
  44.5 1.9 %collective-permute-start.1 = (bf16[3,128,256]{2,1,0:T(8,128)(2,1)S(1)}, bf16[3,128,256]{2,1,0:T(8,128)(2,1)S(1)}, u32[]{:S(2)}, u32[]{:S(2)}) collective-permute-start(bf16[3,128,256]{2,1,0:T(8,128)(2,1)S(1)} %broadcast_select_fusion.3), channel_id=1, source_target_pairs={{0,1},{1,2},{2,3},{3,4},{4,5},{5,6},{6,7},{7,8},{8,9},{9,10},{10,1... | collective-permute-start | bytes 589832 | tf_op jit(solution)/shard_map/ppermute | solution.py:12
  47.4 7.2 %collective-permute-start.3 = (bf16[3,128,256]{1,2,0:T(8,128)(2,1)S(1)}, bf16[3,128,256]{1,2,0:T(8,128)(2,1)S(1)}, u32[]{:S(2)}, u32[]{:S(2)}) collective-permute-start(bf16[3,128,256]{1,2,0:T(8,128)(2,1)S(1)} %broadcast_select_fusion.2), channel_id=1, source_target_pairs={{1,0},{2,1},{3,2},{4,3},{5,4},{6,5},{7,6},{8,7},{9,8},{10,9},{11,1... | collective-permute-start | bytes 589832 | tf_op jit(solution)/shard_map/ppermute | solution.py:12
  54.7 2.1 %collective-permute-done.1 = bf16[3,128,256]{2,1,0:T(8,128)(2,1)S(1)} collective-permute-done((bf16[3,128,256]{2,1,0:T(8,128)(2,1)S(1)}, bf16[3,128,256]{2,1,0:T(8,128)(2,1)S(1)}, u32[]{:S(2)}, u32[]{:S(2)}) %collective-permute-start.1) | collective-permute-done | bytes 196640 | tf_op jit(solution)/shard_map/ppermute | solution.py:12
  56.7 3.3 %bitcast_dynamic-update-slice_fusion = f32[12,128,768]{2,1,0:T(8,128)} fusion(f32[12,128,768]{2,1,0:T(8,128)} %pad.39, bf16[12,3,128,128]{3,1,2,0:T(4,128)(2,1)} %get-tuple-element.56, bf16[3,128,256]{2,1,0:T(8,128)(2,1)S(1)} %collective-permute-done.1), kind=kOutput, calls=%fused_computation.26 | convolution fusion | flops 301989888 | bytes 3342336 | tf_op jit(solution)/shard_map/rlab,lbc->rac/dot_general | solution.py:40
  60.1 3.3 %fusion.23 = f32[12,128,768]{2,1,0:T(8,128)} fusion(f32[12,128,768]{2,1,0:T(8,128)} %bitcast_dynamic-update-slice_fusion, bf16[12,3,128,128]{3,1,2,0:T(4,128)(2,1)S(1)} %copy-done.1, bf16[3,128,256]{1,2,0:T(8,128)(2,1)S(1)} %collective-permute-done.3), kind=kOutput, calls=%fused_computation.25 | convolution fusion | flops 302383104 | bytes 4521984 | tf_op jit(solution)/shard_map/rlab,lbc->rac/dot_general | solution.py:46
  63.3 4.9 %fusion.3 = bf16[12,128,768]{1,2,0:T(8,128)(2,1)} fusion(f32[]{:T(128)} %bitcast.64, bf16[12,128,256]{1,2,0:T(8,128)(2,1)S(1)} %copy-done.4, bf16[12,128,128]{2,1,0:T(8,128)(2,1)S(1)} %copy-done.6, f32[12,128,768]{2,1,0:T(8,128)} %fusion.23), kind=kOutput, calls=%fused_computation.11 | convolution fusion | flops 307888128 | bytes 8257540 | tf_op jit(solution)/shard_map/rab,rbc->rac/dot_general | solution.py:91
  68.3 3.1 %gather_fusion.3 = bf16[3,128,768]{1,2,0:T(8,128)(2,1)} fusion(bf16[12,128,768]{1,2,0:T(8,128)(2,1)} %fusion.3, s32[1024]{0:T(1024)S(1)} %pad_clamp_fusion), kind=kCustom, calls=%fused_computation.3.clone | custom fusion | bytes 1179660 | tf_op jit(solution)/shard_map/jit(_take)/gather | solution.py:97
  71.4 3.1 %gather_fusion.2 = bf16[3,128,768]{1,2,0:T(8,128)(2,1)} fusion(bf16[12,128,768]{1,2,0:T(8,128)(2,1)} %fusion.3, s32[1024]{0:T(1024)S(1)} %pad_clamp_fusion.1), kind=kCustom, calls=%fused_computation.1.clone | custom fusion | bytes 1179660 | tf_op jit(solution)/shard_map/jit(_take)/gather | solution.py:96
  76.9 1.9 %collective-permute-start.4 = (bf16[3,128,768]{1,2,0:T(8,128)(2,1)S(1)}, bf16[3,128,768]{1,2,0:T(8,128)(2,1)S(1)}, u32[]{:S(2)}, u32[]{:S(2)}) collective-permute-start(bf16[3,128,768]{1,2,0:T(8,128)(2,1)S(1)} %broadcast_select_fusion.1), channel_id=1, source_target_pairs={{0,1},{1,2},{2,3},{3,4},{4,5},{5,6},{6,7},{7,8},{8,9},{9,10},{10,1... | collective-permute-start | bytes 1769480 | tf_op jit(solution)/shard_map/ppermute | solution.py:12
  78.8 7.4 %collective-permute-start.5 = (bf16[3,128,768]{1,2,0:T(8,128)(2,1)S(1)}, bf16[3,128,768]{1,2,0:T(8,128)(2,1)S(1)}, u32[]{:S(2)}, u32[]{:S(2)}) collective-permute-start(bf16[3,128,768]{1,2,0:T(8,128)(2,1)S(1)} %broadcast_select_fusion), channel_id=1, source_target_pairs={{1,0},{2,1},{3,2},{4,3},{5,4},{6,5},{7,6},{8,7},{9,8},{10,9},{11,1... | collective-permute-start | bytes 1769480 | tf_op jit(solution)/shard_map/ppermute | solution.py:12
  86.3 7.3 %fusion.16 = f32[12,128,768]{2,1,0:T(8,128)S(1)} fusion(bf16[12,128,768]{1,2,0:T(8,128)(2,1)} %fusion.3, bf16[12,12,128,128]{3,1,2,0:T(8,128)(2,1)} %slice.144), kind=kOutput, calls=%fused_computation.22 | convolution fusion | flops 3623878656 | bytes 11796480 | tf_op jit(solution)/shard_map/rlab,lbc->rac/dot_general | solution.py:34
  94.3 3.1 %collective-permute-done.4 = bf16[3,128,768]{1,2,0:T(8,128)(2,1)S(1)} collective-permute-done((bf16[3,128,768]{1,2,0:T(8,128)(2,1)S(1)}, bf16[3,128,768]{1,2,0:T(8,128)(2,1)S(1)}, u32[]{:S(2)}, u32[]{:S(2)}) %collective-permute-start.4) | collective-permute-done | bytes 589856 | tf_op jit(solution)/shard_map/ppermute | solution.py:12
  97.5 1.6 %fusion.2 = f32[12,128,1280]{2,1,0:T(8,128)S(1)} fusion(f32[12,128,1280]{2,1,0:T(8,128)S(1)} %pad.40, bf16[12,3,128,128]{3,1,2,0:T(4,128)(2,1)S(1)} %copy-done.3, bf16[3,128,768]{1,2,0:T(8,128)(2,1)S(1)} %collective-permute-done.4), kind=kOutput, calls=%fused_computation.9 | convolution fusion | flops 907149312 | bytes 11599872 | tf_op jit(solution)/shard_map/rlab,lbc->rac/dot_general | solution.py:40
  99.2 1.6 %fusion.1 = f32[12,128,1280]{2,1,0:T(8,128)S(1)} fusion(f32[12,128,1280]{2,1,0:T(8,128)S(1)} %fusion.2, bf16[12,3,128,128]{3,1,2,0:T(4,128)(2,1)S(1)} %copy-done.2, bf16[3,128,768]{1,2,0:T(8,128)(2,1)S(1)} %collective-permute-done.5), kind=kOutput, calls=%fused_computation.7 | convolution fusion | flops 907149312 | bytes 11599872 | tf_op jit(solution)/shard_map/rlab,lbc->rac/dot_general | solution.py:46
  100.8 3.3 %fusion.41 = (bf16[768,1280]{1,0:T(8,128)(2,1)S(1)}, f32[768,1280]{1,0:T(8,128)S(1)}) fusion(bf16[12,128,768]{1,2,0:T(8,128)(2,1)S(1)} %copy-done.5, f32[12,128,1280]{2,1,0:T(8,128)S(1)} %fusion.1), kind=kOutput, calls=%fused_computation.56 | convolution fusion | flops 3022848000 | bytes 16121856 | tf_op jit(solution)/shard_map/dot_general | solution.py:104
  104.2 1.9 %collective-permute-start.6 = (bf16[256,1280]{1,0:T(8,128)(2,1)S(1)}, bf16[256,1280]{1,0:T(8,128)(2,1)S(1)}, u32[]{:S(2)}, u32[]{:S(2)}) collective-permute-start(bf16[256,1280]{1,0:T(8,128)(2,1)S(1)} %get-tuple-element.57), channel_id=1, source_target_pairs={{1,0},{2,1},{3,2},{4,3},{5,4},{6,5},{7,6},{8,7},{9,8},{10,9},{11,1... | collective-permute-start | bytes 1966088 | tf_op jit(solution)/shard_map/ppermute | solution.py:12
  106.2 2.4 %collective-permute-start.7 = (bf16[256,1280]{1,0:T(8,128)(2,1)S(1)}, bf16[256,1280]{1,0:T(8,128)(2,1)S(1)}, u32[]{:S(2)}, u32[]{:S(2)}) collective-permute-start(bf16[256,1280]{1,0:T(8,128)(2,1)S(1)} %get-tuple-element.58), channel_id=1, source_target_pairs={{0,1},{1,2},{2,3},{3,4},{4,5},{5,6},{6,7},{7,8},{8,9},{9,10},{10,1... | collective-permute-start | bytes 1966088 | tf_op jit(solution)/shard_map/ppermute | solution.py:12
  108.7 10.9 %collective-permute-done.6 = bf16[256,1280]{1,0:T(8,128)(2,1)S(1)} collective-permute-done((bf16[256,1280]{1,0:T(8,128)(2,1)S(1)}, bf16[256,1280]{1,0:T(8,128)(2,1)S(1)}, u32[]{:S(2)}, u32[]{:S(2)}) %collective-permute-start.6) | collective-permute-done | bytes 655392 | tf_op jit(solution)/shard_map/ppermute | solution.py:12
  119.5 2.4 %collective-permute-done.7 = bf16[256,1280]{1,0:T(8,128)(2,1)S(1)} collective-permute-done((bf16[256,1280]{1,0:T(8,128)(2,1)S(1)}, bf16[256,1280]{1,0:T(8,128)(2,1)S(1)}, u32[]{:S(2)}, u32[]{:S(2)}) %collective-permute-start.7) | collective-permute-done | bytes 655392 | tf_op jit(solution)/shard_map/ppermute | solution.py:12
  (41 shorter events, 8.0 us)
Async XLA Ops:
  0.0 10.6 %copy-start = (bf16[12,9,128,128]{3,2,1,0:T(8,128)(2,1)S(1)}, bf16[12,9,128,128]{3,2,1,0:T(8,128)(2,1)}, u32[]{:S(2)}) copy-start(bf16[12,9,128,128]{3,2,1,0:T(8,128)(2,1)} %param.19) | copy-start | bytes 10616836
  1.4 35.9 %collective-permute-start.2 = (s32[3]{0:T(128)}, s32[3]{0:T(128)S(1)}, u32[]{:S(2)}, u32[]{:S(2)}) collective-permute-start(s32[3]{0:T(128)} %get-tuple-element.59), channel_id=1, source_target_pairs={{0,1},{1,2},{2,3},{3,4},{4,5},{5,6},{6,7},{7,8},{8,9},{9,10},{10,1... | collective-permute-start | bytes 44 | tf_op jit(solution)/shard_map/ppermute | solution.py:12
  3.3 34.0 %collective-permute-start = (s32[3]{0:T(128)S(1)}, s32[3]{0:T(128)S(1)}, u32[]{:S(2)}, u32[]{:S(2)}) collective-permute-start(s32[3]{0:T(128)S(1)} %get-tuple-element.60), channel_id=1, source_target_pairs={{1,0},{2,1},{3,2},{4,3},{5,4},{6,5},{7,6},{8,7},{9,8},{10,9},{11,1... | collective-permute-start | bytes 44 | tf_op jit(solution)/shard_map/ppermute | solution.py:12
  19.1 4.4 %copy-start.7 = (s32[12]{0:T(128)S(1)}, s32[12]{0:T(128)}, u32[]{:S(2)}) copy-start(s32[12]{0:T(128)} %param.23) | copy-start | bytes 148
  37.3 0.6 copy-start.8
  37.9 2.4 %copy-start.9 = (s32[3]{0:T(128)}, s32[3]{0:T(128)S(1)}, u32[]{:S(2)}) copy-start(s32[3]{0:T(128)S(1)} %collective-permute-done) | copy-start | bytes 40
  42.7 17.4 %copy-start.1 = (bf16[12,3,128,128]{3,1,2,0:T(4,128)(2,1)S(1)}, bf16[12,3,128,128]{3,1,2,0:T(4,128)(2,1)}, u32[]{:S(2)}) copy-start(bf16[12,3,128,128]{3,1,2,0:T(4,128)(2,1)} %get-tuple-element.55) | copy-start | bytes 3538948
  44.5 12.3 %collective-permute-start.1 = (bf16[3,128,256]{2,1,0:T(8,128)(2,1)S(1)}, bf16[3,128,256]{2,1,0:T(8,128)(2,1)S(1)}, u32[]{:S(2)}, u32[]{:S(2)}) collective-permute-start(bf16[3,128,256]{2,1,0:T(8,128)(2,1)S(1)} %broadcast_select_fusion.3), channel_id=1, source_target_pairs={{0,1},{1,2},{2,3},{3,4},{4,5},{5,6},{6,7},{7,8},{8,9},{9,10},{10,1... | collective-permute-start | bytes 589832 | tf_op jit(solution)/shard_map/ppermute | solution.py:12
  47.4 12.6 %collective-permute-start.3 = (bf16[3,128,256]{1,2,0:T(8,128)(2,1)S(1)}, bf16[3,128,256]{1,2,0:T(8,128)(2,1)S(1)}, u32[]{:S(2)}, u32[]{:S(2)}) collective-permute-start(bf16[3,128,256]{1,2,0:T(8,128)(2,1)S(1)} %broadcast_select_fusion.2), channel_id=1, source_target_pairs={{1,0},{2,1},{3,2},{4,3},{5,4},{6,5},{7,6},{8,7},{9,8},{10,9},{11,1... | collective-permute-start | bytes 589832 | tf_op jit(solution)/shard_map/ppermute | solution.py:12
  56.7 6.6 %copy-start.4 = (bf16[12,128,256]{1,2,0:T(8,128)(2,1)S(1)}, bf16[12,128,256]{1,2,0:T(8,128)(2,1)}, u32[]{:S(2)}) copy-start(bf16[12,128,256]{1,2,0:T(8,128)(2,1)} %bitcast_select_fusion) | copy-start | bytes 2359300
  56.7 6.6 %copy-start.6 = (bf16[12,128,128]{2,1,0:T(8,128)(2,1)S(1)}, bf16[12,128,128]{2,1,0:T(8,128)(2,1)}, u32[]{:S(2)}) copy-start(bf16[12,128,128]{2,1,0:T(8,128)(2,1)} %param.22) | copy-start | bytes 1179652
  76.9 20.6 %collective-permute-start.4 = (bf16[3,128,768]{1,2,0:T(8,128)(2,1)S(1)}, bf16[3,128,768]{1,2,0:T(8,128)(2,1)S(1)}, u32[]{:S(2)}, u32[]{:S(2)}) collective-permute-start(bf16[3,128,768]{1,2,0:T(8,128)(2,1)S(1)} %broadcast_select_fusion.1), channel_id=1, source_target_pairs={{0,1},{1,2},{2,3},{3,4},{4,5},{5,6},{6,7},{7,8},{8,9},{9,10},{10,1... | collective-permute-start | bytes 1769480 | tf_op jit(solution)/shard_map/ppermute | solution.py:12
  78.8 20.3 %collective-permute-start.5 = (bf16[3,128,768]{1,2,0:T(8,128)(2,1)S(1)}, bf16[3,128,768]{1,2,0:T(8,128)(2,1)S(1)}, u32[]{:S(2)}, u32[]{:S(2)}) collective-permute-start(bf16[3,128,768]{1,2,0:T(8,128)(2,1)S(1)} %broadcast_select_fusion), channel_id=1, source_target_pairs={{1,0},{2,1},{3,2},{4,3},{5,4},{6,5},{7,6},{8,7},{9,8},{10,9},{11,1... | collective-permute-start | bytes 1769480 | tf_op jit(solution)/shard_map/ppermute | solution.py:12
  93.6 3.9 %copy-start.3 = (bf16[12,3,128,128]{3,1,2,0:T(4,128)(2,1)S(1)}, bf16[12,3,128,128]{3,1,2,0:T(4,128)(2,1)}, u32[]{:S(2)}) copy-start(bf16[12,3,128,128]{3,1,2,0:T(4,128)(2,1)} %get-tuple-element.56) | copy-start | bytes 3538948
  94.3 4.8 %copy-start.2 = (bf16[12,3,128,128]{3,1,2,0:T(4,128)(2,1)S(1)}, bf16[12,3,128,128]{3,1,2,0:T(4,128)(2,1)}, u32[]{:S(2)}) copy-start(bf16[12,3,128,128]{3,1,2,0:T(4,128)(2,1)} %get-tuple-element.55) | copy-start | bytes 3538948
  99.1 1.7 %copy-start.5 = (bf16[12,128,768]{1,2,0:T(8,128)(2,1)S(1)}, bf16[12,128,768]{1,2,0:T(8,128)(2,1)}, u32[]{:S(2)}) copy-start(bf16[12,128,768]{1,2,0:T(8,128)(2,1)} %fusion.3) | copy-start | bytes 7077892
  104.2 15.3 %collective-permute-start.6 = (bf16[256,1280]{1,0:T(8,128)(2,1)S(1)}, bf16[256,1280]{1,0:T(8,128)(2,1)S(1)}, u32[]{:S(2)}, u32[]{:S(2)}) collective-permute-start(bf16[256,1280]{1,0:T(8,128)(2,1)S(1)} %get-tuple-element.57), channel_id=1, source_target_pairs={{1,0},{2,1},{3,2},{4,3},{5,4},{6,5},{7,6},{8,7},{9,8},{10,9},{11,1... | collective-permute-start | bytes 1966088 | tf_op jit(solution)/shard_map/ppermute | solution.py:12
  106.2 15.8 %collective-permute-start.7 = (bf16[256,1280]{1,0:T(8,128)(2,1)S(1)}, bf16[256,1280]{1,0:T(8,128)(2,1)S(1)}, u32[]{:S(2)}, u32[]{:S(2)}) collective-permute-start(bf16[256,1280]{1,0:T(8,128)(2,1)S(1)} %get-tuple-element.58), channel_id=1, source_target_pairs={{0,1},{1,2},{2,3},{3,4},{4,5},{5,6},{6,7},{7,8},{8,9},{9,10},{10,1... | collective-permute-start | bytes 1966088 | tf_op jit(solution)/shard_map/ppermute | solution.py:12
where the time goes:
time: 124 us; the launch traced here: 123 us
  matrix products  34.8 us (28%)
  starting transfers between devices  32 us (26%)
  local copies, waits for them, and re-layouts  28.2 us (23%)
  waiting for transfers between devices  18.6 us (15%)
  other arithmetic  8.63 us (7%)
    ppermute x8, starting transfers between devices, from_behind(): return lax.ppermute(block, axis, route)  32 us
    ppermute x8, waiting for transfers between devices, from_behind(): return lax.ppermute(block, axis, route)  18.6 us
    dot_general x2, matrix products, assemble(): jnp.einsum('rlab,lbc->rac', dense[:, :own_count], lookup[:own_count], pre...  11.7 us
    dot_general x1, matrix products, dense_rows(): jnp.einsum('rkl,rkab->rlab', selector, values, preferred_element_type=jnp...  5.08 us
    dot_general x1, matrix products, shards(): jnp.einsum('rab,rbc->rac', inverse_diagonal, smooth_half, preferred_eleme...  4.94 us
    dot_general x2, matrix products, assemble(): jnp.einsum('rlab,lbc->rac', dense[:, own_count:own_count + ghost_count],...  4.94 us
    dot_general x2, matrix products, assemble(): jnp.einsum('rlab,lbc->rac', dense[:, own_count + ghost_count:], lookup[ow...  4.9 us
    slice x1, local copies, waits for them, and re-layouts, assemble(): dense[:, :own_count]  3.76 us
  transfers between devices with their start and end apart: 8, of which 4 were waited for; matrix products, arithmetic and copies ran while one was open for 33% of the time, Pallas kernels for 0%

commit v1 on v0

v1 whole, which is shorter than its diff:
```python
import functools

import jax
import jax.numpy as jnp
from jax import lax
from jax.experimental import pallas as pl
from jax.experimental.pallas import tpu as pltpu
from jax.sharding import PartitionSpec as P

CA = 2
HEAD = 8
LANES = 128
META, TENT, MID, LEFT, RIGHT, PART = 0, 1, 2, 3, 4, 5
MESSAGES = 10


def dot(a, b):
    return jnp.dot(a, b, preferred_element_type=jnp.float32)


def kernel(
    n_grp,
    n_dev,
    damping_ref,
    meta_ref,
    meta_vec,
    values_hbm,
    tent_hbm,
    inv_hbm,
    out_hbm,
    a_raw,
    t_raw,
    d_raw,
    a_own,
    a_side,
    tt,
    stage_t,
    ghost_t,
    meta_in,
    meta_s,
    tg,
    p,
    stage_p,
    ghost_p,
    pt,
    ap,
    own_acc,
    part_send,
    part_recv,
    out_v,
    a_sem,
    local_sem,
    out_sem,
    send_sem,
    recv_sem,
):
    rows, slots, width, _ = values_hbm.shape
    listed = stage_t.shape[1]
    span = CA * width
    group = max(g for g in (1, 2, 3, 4) if rows % g == 0)
    chunk = group * width
    total = n_grp * n_dev
    me = lax.axis_index("grp") * n_dev + lax.axis_index("dev")
    has = (me > 0, me < total - 1)
    other = (lax.rem(me + (total - 1), total), lax.rem(me + 1, total))
    device = [(lax.div(o, n_dev), lax.rem(o, n_dev)) for o in other]

    def message(side, index, source, target):
        return pltpu.make_async_remote_copy(
            src_ref=source,
            dst_ref=target,
            send_sem=send_sem.at[side, index],
            recv_sem=recv_sem.at[1 - side, index],
            device_id=device[side],
            device_id_type=pl.DeviceIdType.MESH,
        )

    def meta_msg(side):
        return message(side, META, meta_vec.at[pl.ds(0, HEAD)], meta_in.at[1 - side])

    def tent_msg(side):
        return message(side, TENT, stage_t.at[side], ghost_t.at[1 - side])

    def p_msg(side, part):
        index = (LEFT, MID, RIGHT)[part]
        return message(side, index, stage_p.at[side, part], ghost_p.at[1 - side, part])

    def part_msg(side, column):
        return message(
            side, PART + column, part_send.at[side, column], part_recv.at[1 - side, column]
        )

    def both(action):
        for side in (0, 1):
            pl.when(has[side])(functools.partial(action, side))

    barrier = pltpu.get_barrier_semaphore()
    both(
        lambda side: pl.semaphore_signal(
            barrier, inc=1, device_id=device[side], device_id_type=pl.DeviceIdType.MESH
        )
    )

    def a_copy(r):
        return pltpu.make_async_copy(
            values_hbm.at[r], a_raw.at[r, pl.ds(0, slots)], a_sem.at[r]
        )

    t_copy = pltpu.make_async_copy(tent_hbm, t_raw, local_sem.at[0])
    d_copy = pltpu.make_async_copy(inv_hbm, d_raw, local_sem.at[1])
    t_copy.start()

    @pl.loop(0, rows)
    def _(r):
        a_copy(r).start()
        a_raw[r, slots] = jnp.zeros((width, width), a_raw.dtype)

    d_copy.start()
    for side in (0, 1):

        @pl.when(jnp.logical_not(has[side]))
        def _():
            tg[side] = jnp.zeros(tg.shape[1:], tg.dtype)
            ghost_p[side] = jnp.zeros(ghost_p.shape[1:], ghost_p.dtype)
            part_recv[side] = jnp.zeros(part_recv.shape[1:], part_recv.dtype)

    pl.semaphore_wait(barrier, has[0].astype(jnp.int32) + has[1].astype(jnp.int32))
    both(lambda side: meta_msg(side).start())

    def placed(block, coarse):
        wide = jnp.concatenate([block] * CA, axis=1)
        at = lax.broadcasted_iota(jnp.int32, wide.shape, 1) // width
        return jnp.where(at == jnp.full(wide.shape, coarse, jnp.int32), wide, 0).astype(block.dtype)

    t_copy.wait()

    @pl.loop(0, rows)
    def _(r):
        tt[pl.ds(pl.multiple_of(r * width, width), width), :] = placed(t_raw[r], meta_ref[2, r])

    def lists_in(side):
        meta_msg(1 - side).wait_recv()
        copy = pltpu.make_async_copy(meta_in.at[side], meta_s.at[side], local_sem.at[2 + side])
        copy.start()
        copy.wait()
        for s in range(listed):
            stage_t[side, s] = t_raw[meta_s[side, 1 - side, s]]
        tent_msg(side).start()

    both(lists_in)

    @pl.loop(0, rows)
    def _(r):
        a_copy(r).wait()

    @pl.loop(0, rows)
    def _(r):
        at = pl.ds(pl.multiple_of(r * width, width), width)
        for l in range(rows):
            a_own[at, l * width : (l + 1) * width] = a_raw[r, meta_ref[HEAD + r, l]]
        for side in (0, 1):
            for s in range(listed):
                a_side[side, at, s * width : (s + 1) * width] = a_raw[
                    r, meta_ref[HEAD + r, rows + side * listed + s]
                ]

    d_copy.wait()
    damping = damping_ref[0]

    def smooth(part, matrix, lookup, keep):
        @pl.loop(0, rows // group)
        def _(g):
            at = pl.ds(pl.multiple_of(g * chunk, chunk), chunk)
            half = dot(matrix[at, :], lookup[...]).astype(jnp.bfloat16)
            for i in range(group):
                r = g * group + i
                here = pl.ds(pl.multiple_of(r * width, width), width)
                scaled = damping * dot(d_raw[r], half[i * width : (i + 1) * width])
                if keep:
                    value = tt[here, :].astype(jnp.float32) - scaled
                else:
                    value = -scaled
                p[part, r] = value.astype(jnp.bfloat16)

    def send_p(part):
        def send(side):
            for s in range(listed):
                stage_p[side, part, s * width : (s + 1) * width, :] = p[
                    part, meta_s[side, 1 - side, s]
                ]
            p_msg(side, part).start()

        both(send)

    smooth(1, a_own, tt, True)
    send_p(1)

    def tent_in(side):
        tent_msg(1 - side).wait_recv()
        for s in range(listed):
            coarse = meta_s[side, 2, meta_ref[side, s]]
            tg[side, s * width : (s + 1) * width, :] = placed(ghost_t[side, s], coarse)

    both(tent_in)
    smooth(0, a_side.at[0], tg.at[0], False)
    send_p(0)
    smooth(2, a_side.at[1], tg.at[1], False)
    send_p(2)

    for part in range(3):

        @pl.loop(0, rows)
        def _(r):
            pt[part, r] = p[part, r].T

    def galerkin(column, terms):
        @pl.loop(0, rows // group)
        def _(g):
            at = pl.ds(pl.multiple_of(g * chunk, chunk), chunk)
            value = None
            for matrix, lookup in terms:
                term = dot(matrix[at, :], lookup[...].reshape(-1, span))
                value = term if value is None else value + term
            ap[at, :] = value.astype(jnp.bfloat16)

        def product(part):
            lhs = jnp.concatenate([pt[part, r] for r in range(rows)], axis=1)
            return dot(lhs, ap[...])

        for side, part in ((0, 0), (1, 2)):
            part_send[side, column] = product(part).astype(jnp.bfloat16)
            pl.when(has[side])(lambda: part_msg(side, column).start())
        own_acc[column] = product(1)

    def p_in(side, part):
        pl.when(has[side])(lambda: p_msg(1 - side, part).wait_recv())

    left, right = a_side.at[0], a_side.at[1]
    p_in(0, 1)
    galerkin(1, [(a_own, p.at[0]), (left, ghost_p.at[0, 1])])
    p_in(1, 1)
    galerkin(3, [(a_own, p.at[2]), (right, ghost_p.at[1, 1])])
    p_in(0, 0)
    galerkin(0, [(left, ghost_p.at[0, 0])])
    p_in(1, 2)
    galerkin(4, [(right, ghost_p.at[1, 2])])
    p_in(0, 2)
    p_in(1, 0)
    galerkin(2, [(a_own, p.at[1]), (left, ghost_p.at[0, 2]), (right, ghost_p.at[1, 0])])

    def out_copy(s):
        return pltpu.make_async_copy(
            out_v.at[s], out_hbm.at[:, :, pl.ds(s * span, span)], out_sem.at[s]
        )

    for s in (1, 5, 3, 0, 6, 2, 4):
        value = None
        if 0 <= s - 1 < 5:
            value = own_acc[s - 1]
        for side, column in ((0, s), (1, s - 2)):
            if 0 <= column < 5:
                pl.when(has[side])(lambda: part_msg(1 - side, column).wait_recv())
                term = part_recv[side, column].astype(jnp.float32)
                value = term if value is None else value + term
        out_v[s] = value.astype(jnp.bfloat16).reshape(CA, width, span)
        out_copy(s).start()

    def finish(side):
        meta_msg(side).wait_send()
        tent_msg(side).wait_send()
        for part in range(3):
            p_msg(side, part).wait_send()
        for column in range(5):
            part_msg(side, column).wait_send()

    both(finish)
    for s in range(7):
        out_copy(s).wait()


def shards(
    n_grp,
    n_dev,
    block_values,
    block_columns,
    tentative,
    inverse_diagonal,
    aggregate,
    ghost_rows,
    damping,
):
    rows, slots = block_columns.shape
    width = tentative.shape[1]
    listed = ghost_rows.shape[2]
    lookups = rows + 2 * listed
    span = CA * width
    slot = jnp.arange(slots, dtype=jnp.int32)[None, :, None] - slots
    match = block_columns[:, :, None] == jnp.arange(LANES, dtype=jnp.int32)[None, None, :]
    place = jnp.sum(jnp.where(match, slot, 0), axis=1, dtype=jnp.int32) + slots
    head = jnp.concatenate(
        [
            jnp.pad(ghost_rows[0], ((0, 0), (0, LANES - listed))),
            jnp.pad(aggregate[None, :], ((0, HEAD - 3), (0, LANES - rows))),
        ],
        axis=0,
    )
    meta = jnp.concatenate([head, place], axis=0)
    bf16, f32 = jnp.bfloat16, jnp.float32
    tall = rows * width
    side = listed * width
    scratch = [
        pltpu.VMEM((rows, slots + 1, width, width), bf16),
        pltpu.VMEM((rows, width, width), bf16),
        pltpu.VMEM((rows, width, width), bf16),
        pltpu.VMEM((tall, tall), bf16),
        pltpu.VMEM((2, tall, side), bf16),
        pltpu.VMEM((tall, span), bf16),
        pltpu.VMEM((2, listed, width, width), bf16),
        pltpu.VMEM((2, listed, width, width), bf16),
        pltpu.VMEM((2, HEAD, LANES), jnp.int32),
        pltpu.SMEM((2, HEAD, LANES), jnp.int32),
        pltpu.VMEM((2, side, span), bf16),
        pltpu.VMEM((3, rows, width, span), bf16),
        pltpu.VMEM((2, 3, side, span), bf16),
        pltpu.VMEM((2, 3, side, span), bf16),
        pltpu.VMEM((3, rows, span, width), bf16),
        pltpu.VMEM((tall, span), bf16),
        pltpu.VMEM((5, span, span), f32),
        pltpu.VMEM((2, 5, span, span), bf16),
        pltpu.VMEM((2, 5, span, span), bf16),
        pltpu.VMEM((7, CA, width, span), bf16),
        pltpu.SemaphoreType.DMA((rows,)),
        pltpu.SemaphoreType.DMA((4,)),
        pltpu.SemaphoreType.DMA((7,)),
        pltpu.SemaphoreType.DMA((2, MESSAGES)),
        pltpu.SemaphoreType.DMA((2, MESSAGES)),
    ]
    flops = 2 * tall * span * (tall * 4 + side * 8 + 15 * span)
    return pl.pallas_call(
        functools.partial(kernel, n_grp, n_dev),
        out_shape=jax.ShapeDtypeStruct((CA, width, 7 * span), bf16),
        in_specs=[
            pl.BlockSpec(memory_space=pltpu.SMEM),
            pl.BlockSpec(memory_space=pltpu.SMEM),
            pl.BlockSpec(memory_space=pltpu.VMEM),
            pl.BlockSpec(memory_space=pl.ANY),
            pl.BlockSpec(memory_space=pl.ANY),
            pl.BlockSpec(memory_space=pl.ANY),
        ],
        out_specs=pl.BlockSpec(memory_space=pl.ANY),
        scratch_shapes=scratch,
        compiler_params=pltpu.CompilerParams(
            collective_id=0, has_side_effects=True, vmem_limit_bytes=48 << 20
        ),
        cost_estimate=pl.CostEstimate(
            flops=flops, bytes_accessed=block_values.size * 2, transcendentals=0
        ),
    )(damping, meta, meta, block_values, tentative, inverse_diagonal)


def solution(mesh):
    return jax.shard_map(
        functools.partial(shards, mesh.shape["grp"], mesh.shape["dev"]),
        mesh=mesh,
        in_specs=(
            P(("grp", "dev"), None, None, None),
            P(("grp", "dev"), None),
            P(("grp", "dev"), None, None),
            P(("grp", "dev"), None, None),
            P(("grp", "dev")),
            P(("grp", "dev"), None, None),
            P(),
        ),
        out_specs=P(("grp", "dev"), None, None),
        check_vma=False,
    )
```

time: 124 us -> 50 us (0.40)
  Pallas kernels: 0 us -> 42.5 us
  matrix products: 34.8 us -> 0 us
  starting transfers between devices: 32 us -> 0 us
  local copies, waits for them, and re-layouts: 28.2 us -> 5.7 us
  waiting for transfers between devices: 18.6 us -> 0 us
  other arithmetic: 8.63 us -> 0.81 us
    pallas_call x0 -> x1, Pallas kernels: none -> 42.5 us  [shards(): pl.pallas_call(functools.partial(kernel, n_grp, n_dev), out_shape=jax.Sha...]
    dot_general x9 -> x0, matrix products: 34.8 us -> none  [the longest x2 11.7 us: assemble(): jnp.einsum('rlab,lbc->rac', dense[:, :own_count], lookup[:own_count], pre...]
    ppermute x8 -> x0, starting transfers between devices: 32 us -> none  [from_behind(): return lax.ppermute(block, axis, route)]
    ppermute x8 -> x0, waiting for transfers between devices: 18.6 us -> none  [from_behind(): return lax.ppermute(block, axis, route)]
    gather x4 -> x0, local copies, waits for them, and re-layouts: 11 us -> none  [the longest x1 3.14 us: shards(): right_smoothed = rim_smoothed(jnp.take(prolong, wanted_left, axis=0), -1)]
    slice x4 -> x0, local copies, waits for them, and re-layouts: 7.38 us -> none  [the longest x1 3.76 us: assemble(): dense[:, :own_count]]
    select_n x7 -> x0, other arithmetic: 6.65 us -> none  [the longest x1 2.24 us: place_own(): jnp.where(aggregate_mask[:, None, :, None], tentative[:, :, None, :], jnp...]
    pad x2 -> x0, local copies, waits for them, and re-layouts: 3.46 us -> none  [assemble(): total = jnp.pad(middle, ((0, 0), (0, 0), (block_span, block_span)))]
  transfers between devices with their start and end apart: 8 -> 0, of which waited for: 4 -> 0; matrix products, arithmetic and copies ran while one was open for 33% -> 0% of each run, Pallas kernels for 0% -> 0%
where the time goes in v1:
time: 50 us; the launch traced here: 49.7 us
  Pallas kernels  42.5 us (85%)
  local copies, waits for them, and re-layouts  5.7 us (11%)
  other arithmetic  0.81 us (2%)
  between operations  0.69 us (1%)
    pallas_call x1, Pallas kernels, shards(): pl.pallas_call(functools.partial(kernel, n_grp, n_dev), out_shape=jax.Sha...  42.5 us
    unnamed x8, local copies, waits for them, and re-layouts  5.7 us

profile of v1, /device:TPU:4, one launch (start us, length us, event | category | flops | bytes accessed | tf_op | source)
XLA Modules:
  0.0 49.7 jit_solution(9013940640767823539)
XLA Ops:
  0.7 0.8 %copy.8 = s32[12,9]{0,1:T(8,128)S(1)} copy(s32[12,9]{1,0:T(8,128)} %param.8) | data formatting | bytes 864 | tf_op args[1]
  1.4 0.1 select_reduce_fusion
  1.6 0.7 %fusion.meta_ref.meta_vec = s32[20,128]{1,0:T(8,128)S(1)} fusion(s32[1,12]{1,0:T(1,128)} %bitcast.3, s32[2,3]{1,0:T(2,128)} %bitcast.2, s32[12,128]{1,0:T(8,128)S(1)} %broadcast_add_fusion), kind=kLoop, calls=%fused_computation.3 | loop fusion | flops 5120 | bytes 16456 | tf_op jit(solution)/shard_map/concatenate | solution.py:307
  2.3 0.0 copy-start
  2.3 2.0 %copy-done = bf16[12,9,128,128]{3,2,1,0:T(8,128)(2,1)S(1)} copy-done((bf16[12,9,128,128]{3,2,1,0:T(8,128)(2,1)S(1)}, bf16[12,9,128,128]{3,2,1,0:T(8,128)(2,1)}, u32[]{:S(2)}) %copy-start) | copy-done | bytes 3538968
  4.3 0.0 copy-start.1
  4.3 1.0 %copy-done.1 = bf16[12,128,128]{2,1,0:T(8,128)(2,1)S(1)} copy-done((bf16[12,128,128]{2,1,0:T(8,128)(2,1)S(1)}, bf16[12,128,128]{2,1,0:T(8,128)(2,1)}, u32[]{:S(2)}) %copy-start.1) | copy-done | bytes 393240
  5.3 0.0 copy-start.2
  5.3 1.0 %copy-done.2 = bf16[12,128,128]{2,1,0:T(8,128)(2,1)S(1)} copy-done((bf16[12,128,128]{2,1,0:T(8,128)(2,1)S(1)}, bf16[12,128,128]{2,1,0:T(8,128)(2,1)}, u32[]{:S(2)}) %copy-start.2) | copy-done | bytes 393240
  6.3 42.5 %shard_map.73 = bf16[2,128,1792]{2,1,0:T(8,128)(2,1)S(1)} custom-call(f32[1]{0:T(128)S(6)} %copy.10.damping_ref, s32[20,128]{1,0:T(8,128)S(1)} %fusion.meta_ref.meta_vec, s32[20,128]{1,0:T(8,128)S(1)} %fusion.meta_ref.meta_vec, bf16[12,9,128,128]{3,2,1,0:T(8,128)(2,1)S(1)} %copy-done, bf16[12,128,128]{2,1,0:T(8,128)(2,1)S(1)} %copy-done.1, ...), custom_call_target="tpu_custom_call" | custom-call | flops 10267656192 | bytes 3538944 | tf_op jit(solution)/shard_map/pallas_call | solution.py:339
  48.7 0.9 %copy.11 = bf16[2,128,1792]{2,1,0:T(8,128)(2,1)} copy(bf16[2,128,1792]{2,1,0:T(8,128)(2,1)S(1)} %shard_map.73) | data formatting | bytes 1835008
  (2 shorter events, 0.0 us)
Async XLA Ops:
  2.3 2.0 %copy-start = (bf16[12,9,128,128]{3,2,1,0:T(8,128)(2,1)S(1)}, bf16[12,9,128,128]{3,2,1,0:T(8,128)(2,1)}, u32[]{:S(2)}) copy-start(bf16[12,9,128,128]{3,2,1,0:T(8,128)(2,1)} %values_hbm.1) | copy-start | bytes 10616836
  4.3 1.0 %copy-start.1 = (bf16[12,128,128]{2,1,0:T(8,128)(2,1)S(1)}, bf16[12,128,128]{2,1,0:T(8,128)(2,1)}, u32[]{:S(2)}) copy-start(bf16[12,128,128]{2,1,0:T(8,128)(2,1)} %tent_hbm.1) | copy-start | bytes 1179652
  5.3 1.0 %copy-start.2 = (bf16[12,128,128]{2,1,0:T(8,128)(2,1)S(1)}, bf16[12,128,128]{2,1,0:T(8,128)(2,1)}, u32[]{:S(2)}) copy-start(bf16[12,128,128]{2,1,0:T(8,128)(2,1)} %inv_hbm.1) | copy-start | bytes 1179652

commit v2 on v1

--- a/solution.py
+++ b/solution.py
@@ -22,12 +22,15 @@
     n_grp,
     n_dev,
     damping_ref,
-    meta_ref,
-    meta_vec,
+    columns_ref,
+    aggregate_ref,
+    ghost_ref,
     values_hbm,
     tent_hbm,
     inv_hbm,
     out_hbm,
+    meta_vec,
+    meta_ref,
     a_raw,
     t_raw,
     d_raw,
@@ -116,6 +119,15 @@
         a_raw[r, slots] = jnp.zeros((width, width), a_raw.dtype)
 
     d_copy.start()
+    lane = lax.broadcasted_iota(jnp.int32, (rows, LANES), 1)
+    place = jnp.full((rows, LANES), slots, jnp.int32)
+    for k in range(slots):
+        place = jnp.where(columns_ref[:, k : k + 1] == lane, k, place)
+    meta_vec[0:2, 0:listed] = ghost_ref[...]
+    meta_vec[2:3, 0:rows] = aggregate_ref[...]
+    meta_vec[HEAD : HEAD + rows, :] = place
+    m_copy = pltpu.make_async_copy(meta_vec, meta_ref, local_sem.at[4])
+    m_copy.start()
     for side in (0, 1):
 
         @pl.when(jnp.logical_not(has[side]))
@@ -133,6 +145,7 @@
         return jnp.where(at == jnp.full(wide.shape, coarse, jnp.int32), wide, 0).astype(block.dtype)
 
     t_copy.wait()
+    m_copy.wait()
 
     @pl.loop(0, rows)
     def _(r):
@@ -292,23 +305,13 @@
     rows, slots = block_columns.shape
     width = tentative.shape[1]
     listed = ghost_rows.shape[2]
-    lookups = rows + 2 * listed
     span = CA * width
-    slot = jnp.arange(slots, dtype=jnp.int32)[None, :, None] - slots
-    match = block_columns[:, :, None] == jnp.arange(LANES, dtype=jnp.int32)[None, None, :]
-    place = jnp.sum(jnp.where(match, slot, 0), axis=1, dtype=jnp.int32) + slots
-    head = jnp.concatenate(
-        [
-            jnp.pad(ghost_rows[0], ((0, 0), (0, LANES - listed))),
-            jnp.pad(aggregate[None, :], ((0, HEAD - 3), (0, LANES - rows))),
-        ],
-        axis=0,
-    )
-    meta = jnp.concatenate([head, place], axis=0)
     bf16, f32 = jnp.bfloat16, jnp.float32
     tall = rows * width
     side = listed * width
     scratch = [
+        pltpu.VMEM((HEAD + rows, LANES), jnp.int32),
+        pltpu.SMEM((HEAD + rows, LANES), jnp.int32),
         pltpu.VMEM((rows, slots + 1, width, width), bf16),
         pltpu.VMEM((rows, width, width), bf16),
         pltpu.VMEM((rows, width, width), bf16),
@@ -330,7 +333,7 @@
         pltpu.VMEM((2, 5, span, span), bf16),
         pltpu.VMEM((7, CA, width, span), bf16),
         pltpu.SemaphoreType.DMA((rows,)),
-        pltpu.SemaphoreType.DMA((4,)),
+        pltpu.SemaphoreType.DMA((5,)),
         pltpu.SemaphoreType.DMA((7,)),
         pltpu.SemaphoreType.DMA((2, MESSAGES)),
         pltpu.SemaphoreType.DMA((2, MESSAGES)),
@@ -341,7 +344,8 @@
         out_shape=jax.ShapeDtypeStruct((CA, width, 7 * span), bf16),
         in_specs=[
             pl.BlockSpec(memory_space=pltpu.SMEM),
-            pl.BlockSpec(memory_space=pltpu.SMEM),
+            pl.BlockSpec(memory_space=pltpu.VMEM),
+            pl.BlockSpec(memory_space=pltpu.VMEM),
             pl.BlockSpec(memory_space=pltpu.VMEM),
             pl.BlockSpec(memory_space=pl.ANY),
             pl.BlockSpec(memory_space=pl.ANY),
@@ -350,12 +354,20 @@
         out_specs=pl.BlockSpec(memory_space=pl.ANY),
         scratch_shapes=scratch,
         compiler_params=pltpu.CompilerParams(
-            collective_id=0, has_side_effects=True, vmem_limit_bytes=48 << 20
+            collective_id=0, has_side_effects=True, vmem_limit_bytes=60 << 20
         ),
         cost_estimate=pl.CostEstimate(
             flops=flops, bytes_accessed=block_values.size * 2, transcendentals=0
         ),
-    )(damping, meta, meta, block_values, tentative, inverse_diagonal)
+    )(
+        damping,
+        block_columns,
+        aggregate[None, :],
+        ghost_rows[0],
+        block_values,
+        tentative,
+        inverse_diagonal,
+    )
 
 
 def solution(mesh):

time: 50 us -> 46.1 us (0.922)
  local copies, waits for them, and re-layouts: 5.7 us -> 2.16 us
  other arithmetic: 0.81 us -> 0 us
  Pallas kernels: 42.5 us -> 43.1 us
    unnamed x8 -> x1, local copies, waits for them, and re-layouts: 5.7 us -> 2.16 us
    concatenate x1 -> x0, other arithmetic: 0.71 us -> none  [shards(): meta = jnp.concatenate([head, place], axis=0)]
    pallas_call x1, Pallas kernels: 42.5 us -> 43.1 us  [shards(): pl.pallas_call(functools.partial(kernel, n_grp, n_dev), out_shape=jax.Sha...]
where the time goes in v2:
time: 46.1 us; the launch traced here: 45.9 us
  Pallas kernels  43.1 us (93%)
  local copies, waits for them, and re-layouts  2.16 us (5%)
  between operations  0.66 us (1%)
    pallas_call x1, Pallas kernels, shards(): pl.pallas_call(functools.partial(kernel, n_grp, n_dev), out_shape=jax.Sha...  43.1 us
    unnamed x1, local copies, waits for them, and re-layouts  2.16 us

profile of v2, /device:TPU:4, one launch (start us, length us, event | category | flops | bytes accessed | tf_op | source)
XLA Modules:
  0.0 45.9 jit_solution(10390825002747379466)
XLA Ops:
  0.7 43.1 %shard_map.73 = bf16[2,128,1792]{2,1,0:T(8,128)(2,1)} custom-call(f32[1]{0:T(128)S(6)} %copy.9.damping_ref, s32[12,9]{1,0:T(8,128)} %columns_ref.1, s32[1,12]{1,0:T(1,128)} %bitcast.3, s32[2,3]{1,0:T(2,128)} %bitcast.2, bf16[12,9,128,128]{3,2,1,0:T(8,128)(2,1)} %values_hbm.1, bf16[12,128,128]{2,1,0:T(8,128)(2,1)} %tent_hbm.1, bf16[12,128,128]{2,1,0:T(8,128)(2,1)} %inv_hbm.1), custom_call_target="tpu_custom_call" | custom-call | flops 10267656192 | bytes 3538944 | tf_op jit(solution)/shard_map/pallas_call | solution.py:342
  43.7 2.2 %copy.10 = bf16[2,128,1792]{2,1,0:T(8,128)(2,1)} copy(bf16[2,128,1792]{2,1,0:T(8,128)(2,1)} %shard_map.73) | data formatting | bytes 1835008

commit v3 on v2

--- a/solution.py
+++ b/solution.py
@@ -47,6 +47,7 @@
     ghost_p,
     pt,
     ap,
+    base,
     own_acc,
     part_send,
     part_recv,
@@ -151,17 +152,6 @@
     def _(r):
         tt[pl.ds(pl.multiple_of(r * width, width), width), :] = placed(t_raw[r], meta_ref[2, r])
 
-    def lists_in(side):
-        meta_msg(1 - side).wait_recv()
-        copy = pltpu.make_async_copy(meta_in.at[side], meta_s.at[side], local_sem.at[2 + side])
-        copy.start()
-        copy.wait()
-        for s in range(listed):
-            stage_t[side, s] = t_raw[meta_s[side, 1 - side, s]]
-        tent_msg(side).start()
-
-    both(lists_in)
-
     @pl.loop(0, rows)
     def _(r):
         a_copy(r).wait()
@@ -177,8 +167,19 @@
                     r, meta_ref[HEAD + r, rows + side * listed + s]
                 ]
 
+    def lists_in(side):
+        meta_msg(1 - side).wait_recv()
+        copy = pltpu.make_async_copy(meta_in.at[side], meta_s.at[side], local_sem.at[2 + side])
+        copy.start()
+        copy.wait()
+        for s in range(listed):
+            stage_t[side, s] = t_raw[meta_s[side, 1 - side, s]]
+        tent_msg(side).start()
+
+    both(lists_in)
+
     d_copy.wait()
-    damping = damping_ref[0]
+    damping = damping_ref[...]
 
     def smooth(part, matrix, lookup, keep):
         @pl.loop(0, rows // group)
@@ -226,13 +227,19 @@
         def _(r):
             pt[part, r] = p[part, r].T
 
+    def ahead(column, part):
+        @pl.loop(0, rows // group)
+        def _(g):
+            at = pl.ds(pl.multiple_of(g * chunk, chunk), chunk)
+            base[column - 1, at, :] = dot(a_own[at, :], p[part].reshape(-1, span))
+
     def galerkin(column, terms):
         @pl.loop(0, rows // group)
         def _(g):
             at = pl.ds(pl.multiple_of(g * chunk, chunk), chunk)
-            value = None
+            value = base[column - 1, at, :] if 1 <= column <= 3 else None
             for matrix, lookup in terms:
-                term = dot(matrix[at, :], lookup[...].reshape(-1, span))
+                term = dot(matrix[at, :], lookup[...])
                 value = term if value is None else value + term
             ap[at, :] = value.astype(jnp.bfloat16)
 
@@ -249,17 +256,20 @@
         pl.when(has[side])(lambda: p_msg(1 - side, part).wait_recv())
 
     left, right = a_side.at[0], a_side.at[1]
+    ahead(1, 0)
+    ahead(3, 2)
     p_in(0, 1)
-    galerkin(1, [(a_own, p.at[0]), (left, ghost_p.at[0, 1])])
+    galerkin(1, [(left, ghost_p.at[0, 1])])
     p_in(1, 1)
-    galerkin(3, [(a_own, p.at[2]), (right, ghost_p.at[1, 1])])
+    galerkin(3, [(right, ghost_p.at[1, 1])])
+    ahead(2, 1)
     p_in(0, 0)
     galerkin(0, [(left, ghost_p.at[0, 0])])
     p_in(1, 2)
     galerkin(4, [(right, ghost_p.at[1, 2])])
     p_in(0, 2)
     p_in(1, 0)
-    galerkin(2, [(a_own, p.at[1]), (left, ghost_p.at[0, 2]), (right, ghost_p.at[1, 0])])
+    galerkin(2, [(left, ghost_p.at[0, 2]), (right, ghost_p.at[1, 0])])
 
     def out_copy(s):
         return pltpu.make_async_copy(
@@ -328,6 +338,7 @@
         pltpu.VMEM((2, 3, side, span), bf16),
         pltpu.VMEM((3, rows, span, width), bf16),
         pltpu.VMEM((tall, span), bf16),
+        pltpu.VMEM((3, tall, span), f32),
         pltpu.VMEM((5, span, span), f32),
         pltpu.VMEM((2, 5, span, span), bf16),
         pltpu.VMEM((2, 5, span, span), bf16),
@@ -343,7 +354,7 @@
         functools.partial(kernel, n_grp, n_dev),
         out_shape=jax.ShapeDtypeStruct((CA, width, 7 * span), bf16),
         in_specs=[
-            pl.BlockSpec(memory_space=pltpu.SMEM),
+            pl.BlockSpec(memory_space=pltpu.VMEM),
             pl.BlockSpec(memory_space=pltpu.VMEM),
             pl.BlockSpec(memory_space=pltpu.VMEM),
             pl.BlockSpec(memory_space=pltpu.VMEM),
@@ -360,7 +371,7 @@
             flops=flops, bytes_accessed=block_values.size * 2, transcendentals=0
         ),
     )(
-        damping,
+        damping[None, :],
         block_columns,
         aggregate[None, :],
         ghost_rows[0],

time: 46.1 us -> 45.9 us (level)
  no operation moved by 1% of the time
where the time goes in v3:
time: 45.9 us; the launch traced here: 45.7 us
  Pallas kernels  42.9 us (93%)
  local copies, waits for them, and re-layouts  2.16 us (5%)
  between operations  0.66 us (1%)
    pallas_call x1, Pallas kernels, shards(): pl.pallas_call(functools.partial(kernel, n_grp, n_dev), out_shape=jax.Sha...  42.9 us
    unnamed x1, local copies, waits for them, and re-layouts  2.16 us

profile of v3, /device:TPU:4, one launch (start us, length us, event | category | flops | bytes accessed | tf_op | source)
XLA Modules:
  0.0 45.7 jit_solution(13689212728622345797)
XLA Ops:
  0.7 42.9 %shard_map.73 = bf16[2,128,1792]{2,1,0:T(8,128)(2,1)} custom-call(f32[1,1]{1,0:T(1,128)} %bitcast.3.damping_ref, s32[12,9]{1,0:T(8,128)} %columns_ref.1, s32[1,12]{1,0:T(1,128)} %bitcast.5, s32[2,3]{1,0:T(2,128)} %bitcast.4, bf16[12,9,128,128]{3,2,1,0:T(8,128)(2,1)} %values_hbm.1, bf16[12,128,128]{2,1,0:T(8,128)(2,1)} %tent_hbm.1, bf16[12,128,128]{2,1,0:T(8,128)(2,1)} %inv_hbm.1), custom_call_target="tpu_custom_call" | custom-call | flops 10267656192 | bytes 3538944 | tf_op jit(solution)/shard_map/pallas_call | solution.py:353
  43.6 2.2 %copy.10 = bf16[2,128,1792]{2,1,0:T(8,128)(2,1)} copy(bf16[2,128,1792]{2,1,0:T(8,128)(2,1)} %shard_map.73) | data formatting | bytes 1835008
